TPU v7x, 32 devices: a whole 2x2x4 slice. The times are simulated.
32 devices in a mesh: row: 8 (over z, x), col: 4 (over y, core).
Axes of the slice: x: 2, y: 2, z: 4, core: 2. Of those that a mesh axis runs over, the one named last changes fastest.
Arguments:
- corner: bfloat16 [8, 4, 64, 64], P('row', 'col'), may hold values from -0.75 to 0.75
- top_edge: bfloat16 [8, 4, 64, 1024], P('row', 'col'), may hold values from -0.75 to 0.75
- left_edge: bfloat16 [8, 4, 64, 1024], P('row', 'col'), may hold values from -0.75 to 0.75
- site_tensor: bfloat16 [8, 4, 2, 4, 4, 4, 4], P('row', 'col'), may hold values from -1.3984375 to 1.3984375
- sketch: bfloat16 [8, 4, 64, 1024], P('row', 'col'), may hold values from -0.1875 to 0.1875
- grad_left: bfloat16 [8, 4, 64, 1024], P('row', 'col'), may hold values from -0.019897461 to 0.019897461
- grad_top: bfloat16 [8, 4, 64, 1024], P('row', 'col'), may hold values from -0.019897461 to 0.019897461
Outputs:
- corner_grad: bfloat16 [8, 4, 64, 64], P('row', 'col')
- top_grad: bfloat16 [8, 4, 64, 1024], P('row', 'col')
- left_grad: bfloat16 [8, 4, 64, 1024], P('row', 'col')
- site_grad: float32 [8, 4, 2, 4, 4, 4, 4], P('row', 'col')
All inputs are finite; a program needn't handle non-finite values.
Results may differ from a plain program's by a relative error of at most 0.014.
Values may be sent and summed in bfloat16 or wider, within the bound.
A program may use at most 64 MiB of HBM per device.

v0:
```python
import functools

import jax
import jax.numpy as jnp
from jax import lax
from jax.experimental import pallas as pl
from jax.experimental.pallas import tpu as pltpu
from jax.sharding import PartitionSpec as P

MESH = pl.DeviceIdType.MESH
F32 = jnp.float32
BF16 = jnp.bfloat16


def mm(a, b):
    return lax.dot_general(a, b, (((1,), (0,)), ((), ())), preferred_element_type=F32)


def mm_nt(a, b):
    return lax.dot_general(a, b, (((1,), (1,)), ((), ())), preferred_element_type=F32)


def edge_rows(x, scr, legs, chi):
    half = chi // 2
    x = x.astype(F32)
    scr[...] = jnp.concatenate([x, pltpu.roll(x, legs * chi - half, 1)], axis=0).T
    parts = [scr[pl.ds(m, legs, stride=chi), :] for m in range(half)]
    return jnp.concatenate(parts, axis=0)


def edge_lanes(p, scr, legs, chi):
    half = chi // 2
    for m in range(half):
        scr[pl.ds(m, legs, stride=chi), :] = p[m * legs : (m + 1) * legs, :]
    x = scr[...].T
    low = lax.rem(lax.broadcasted_iota(jnp.int32, (chi, legs * chi), 1), chi) < half
    return jnp.where(low, x[:chi], pltpu.roll(x[chi:], half, 1))


def spread(x, dst, row, legs, chi):
    two = 2 * chi
    x = x.astype(F32)
    low = lax.broadcasted_iota(jnp.int32, (chi, two), 1) < chi
    for j in range(legs // 2):
        tile = x[:, j * two : (j + 1) * two]
        turned = pltpu.roll(tile, chi, 1)
        for odd, (lo, hi) in enumerate(((tile, turned), (turned, tile))):
            cols = slice((2 * j + odd) * two, (2 * j + odd + 1) * two)
            dst[row : row + chi, cols] = jnp.where(low, lo, 0.0).astype(BF16)
            dst[row + chi : row + two, cols] = jnp.where(low, 0.0, hi).astype(BF16)


def gather_diag(x, legs, chi):
    two = 2 * chi
    low = lax.broadcasted_iota(jnp.int32, (chi, two), 1) < chi
    out = []
    for j in range(legs // 2):
        even = x[:, 2 * j * two : (2 * j + 1) * two]
        odd = x[:, (2 * j + 1) * two : (2 * j + 2) * two]
        left = even[:chi] + pltpu.roll(even[chi:], chi, 1)
        right = pltpu.roll(odd[:chi], chi, 1) + odd[chi:]
        out.append(jnp.where(low, left, right))
    return jnp.concatenate(out, axis=1)


def to_blocks(x, legs, two):
    count = x.shape[0] // legs
    return jnp.concatenate(
        [
            jnp.concatenate(
                [x[m * legs : (m + 1) * legs, u * two : (u + 1) * two] for u in range(legs)], axis=0
            )
            for m in range(count)
        ],
        axis=1,
    )


def to_rows(b, legs, two):
    count = b.shape[1] // two
    return jnp.concatenate(
        [
            jnp.concatenate(
                [b[u * legs : (u + 1) * legs, m * two : (m + 1) * two] for u in range(legs)], axis=1
            )
            for m in range(count)
        ],
        axis=0,
    )


def picks(bond, which, across):
    legs = bond * bond
    full = legs * legs
    shape = (legs, full) if across else (full, legs)
    r = lax.broadcasted_iota(jnp.int32, shape, 1 if across else 0)
    key = lax.broadcasted_iota(jnp.int32, shape, 0 if across else 1)
    hi, lo = r // legs, lax.rem(r, legs)
    if which == 0:
        got = (hi // bond) * bond + lo // bond
    else:
        got = lax.rem(hi, bond) * bond + lax.rem(lo, bond)
    return jnp.where(got == key, 1.0, 0.0).astype(BF16)


def kernel(
    sizes,
    c_ref, u_ref, l_ref, t_ref, sk_ref, gl_ref, gt_ref,
    corner_out, top_out, left_out, site_out,
    lp_own, lp, top_in, corner_in,
    sk_p, sk_n, right_p, down_p,
    skr_in, skb_in, right_in, down_in,
    dtop, dcorner, dleft,
    dtop_in, dcorner_in, dleft_in,
    scr, fbd, rf, lf, a_ref, at_ref, layer,
    secb, qrows, dqb, dsrows,
    send, recv,
):
    chi, bond, phys, chunk = sizes
    legs = bond * bond
    two = 2 * chi
    half = chi // 2
    nr, nc = lax.axis_size("row"), lax.axis_size("col")
    r, c = lax.axis_index("row"), lax.axis_index("col")
    rn, rp = lax.rem(r + 1, nr), lax.rem(r + nr - 1, nr)
    cn, cp = lax.rem(c + 1, nc), lax.rem(c + nc - 1, nc)

    barrier = pltpu.get_barrier_semaphore()
    others = ((rn, c), (rp, c), (r, cn), (r, cp), (rn, cn), (rp, cp))
    for other in others:
        pl.semaphore_signal(barrier, inc=1, device_id=other, device_id_type=MESH)
    lp_own[...] = edge_rows(l_ref[...], scr, legs, chi).astype(BF16)
    pl.semaphore_wait(barrier, len(others))

    def put(n, src, dst, to):
        copy = pltpu.make_async_remote_copy(
            src_ref=src, dst_ref=dst, send_sem=send.at[n], recv_sem=recv.at[n],
            device_id=to, device_id_type=MESH,
        )
        copy.start()
        return copy

    top_copy = put(0, u_ref, top_in, (rn, c))
    corner_copy = put(1, c_ref, corner_in, (rn, cn))
    left_copy = put(2, lp_own, lp, (r, cn))

    for p in range(phys):
        site = t_ref[p * legs : (p + 1) * legs, :]
        for which in range(2):
            wide = mm(site, picks(bond, which, True)).astype(BF16)
            layer[p, which] = mm(picks(bond, which, False), wide).astype(BF16)
    double = sum(
        layer[p, 0].astype(F32) * layer[p, 1].astype(F32) for p in range(phys)
    )
    at_ref[...] = double.astype(BF16)
    a_ref[...] = double.T.astype(BF16)
    spread(gt_ref[...], rf, two, legs, chi)
    spread(sk_ref[...], rf, 2 * two, legs, chi)
    glp = edge_rows(gl_ref[...], scr, legs, chi)
    lf[:, :two] = glp.astype(BF16)
    glp_t = glp.T.astype(BF16)

    top_copy.wait()
    corner_copy.wait()
    first = mm(corner_in[...], top_in[...]).astype(BF16)
    spread(first, fbd, 0, legs, chi)
    left_copy.wait()

    rows_step = chunk * legs
    lanes_step = chunk * two
    steps = half // chunk

    @pl.loop(0, steps)
    def _(n):
        rows = pl.ds(pl.multiple_of(n * rows_step, rows_step), rows_step)
        lanes = pl.ds(pl.multiple_of(n * lanes_step, lanes_step), lanes_step)
        block = to_blocks(mm(lp[rows, :], fbd[...]).astype(BF16), legs, two)
        secb[:, lanes] = block
        qrows[rows, :] = to_rows(mm(a_ref[...], block).astype(BF16), legs, two)

    both = mm_nt(qrows[...], rf[two:, :]).astype(BF16)
    right_p[...] = both[:, :two]
    sk_p[...] = both[:, two:]
    skr_copy = put(3, sk_p, skr_in, (r, cp))
    right_copy = put(5, right_p, right_in, (r, cn))
    sk_n[...] = edge_lanes(both[:, two:].astype(F32), scr, legs, chi).astype(BF16)
    skb_copy = put(4, sk_n, skb_in, (rp, c))
    down = gather_diag(mm(glp_t, qrows[...]), legs, chi).astype(BF16)
    down_p[...] = edge_rows(down, scr, legs, chi).astype(BF16)
    down_copy = put(6, down_p, down_in, (rn, c))

    lp_t = lp[...].astype(F32).T.astype(BF16)
    skr_copy.wait()
    lf[:, two : 2 * two] = skr_in[...]
    skb_copy.wait()
    spread(skb_in[...], rf, 0, legs, chi)
    right_copy.wait()
    down_copy.wait()
    lf[:, 2 * two :] = (down_in[...].astype(F32) + right_in[...].astype(F32)).astype(BF16)

    @pl.loop(0, steps)
    def _(n):
        rows = pl.ds(pl.multiple_of(n * rows_step, rows_step), rows_step)
        lanes = pl.ds(pl.multiple_of(n * lanes_step, lanes_step), lanes_step)
        block = to_blocks(mm(lf[rows, :], rf[...]).astype(BF16), legs, two)
        dqb[:, lanes] = block
        dsrows[rows, :] = to_rows(mm(at_ref[...], block).astype(BF16), legs, two)

    dfirst = gather_diag(mm(lp_t, dsrows[...]), legs, chi).astype(BF16)
    dtop[...] = mm(corner_in[...].astype(F32).T.astype(BF16), dfirst).astype(BF16)
    dtop_copy = put(7, dtop, dtop_in, (rp, c))
    dcorner[...] = mm_nt(dfirst, top_in[...]).astype(BF16)
    dcorner_copy = put(8, dcorner, dcorner_in, (rp, cp))
    dleft[...] = edge_lanes(mm_nt(dsrows[...], fbd[...]), scr, legs, chi).astype(BF16)
    dleft_copy = put(9, dleft, dleft_in, (r, cp))

    ddouble = mm_nt(secb[...], dqb[...])
    for p in range(phys):
        total = None
        for which in range(2):
            part = (ddouble * layer[p, 1 - which].astype(F32)).astype(BF16)
            part = mm(picks(bond, which, True), part).astype(BF16)
            part = mm(part, picks(bond, which, False))
            total = part if total is None else total + part
        site_out[p * legs : (p + 1) * legs, :] = total

    dtop_copy.wait()
    top_out[...] = dtop_in[...]
    dcorner_copy.wait()
    corner_out[...] = dcorner_in[...]
    dleft_copy.wait()
    left_out[...] = dleft_in[...]


def local(corner, top_edge, left_edge, site_tensor, sketch, grad_left, grad_top):
    chi = corner.shape[2]
    phys, bond = site_tensor.shape[2:4]
    legs = bond * bond
    width = legs * chi
    two = 2 * chi
    rows = legs * chi // 2
    wide = legs * two
    full = legs * legs
    vm = lambda *shape: pltpu.VMEM(shape, BF16)
    edge = vm(chi, width)
    packed = vm(rows, two)
    tile = vm(chi, chi)
    spec = pl.BlockSpec(memory_space=pltpu.VMEM)
    outs = pl.pallas_call(
        functools.partial(kernel, (chi, bond, phys, 8)),
        out_shape=(
            jax.ShapeDtypeStruct((chi, chi), BF16),
            jax.ShapeDtypeStruct((chi, width), BF16),
            jax.ShapeDtypeStruct((chi, width), BF16),
            jax.ShapeDtypeStruct((phys * legs, legs), F32),
        ),
        in_specs=[spec] * 7,
        out_specs=(spec,) * 4,
        scratch_shapes=[
            packed, packed, edge, tile,
            packed, edge, packed, packed,
            packed, edge, packed, packed,
            edge, tile, edge,
            edge, tile, edge,
            pltpu.VMEM((width, two), F32),
            vm(two, wide), vm(3 * two, wide), vm(rows, 3 * two),
            vm(full, full), vm(full, full), vm(phys, 2, full, full),
            vm(full, rows * two // legs), vm(rows, wide), vm(full, rows * two // legs), vm(rows, wide),
            pltpu.SemaphoreType.DMA((10,)),
            pltpu.SemaphoreType.DMA((10,)),
        ],
        compiler_params=pltpu.CompilerParams(
            collective_id=0, has_side_effects=True, vmem_limit_bytes=48 * 1024 * 1024
        ),
    )(
        corner[0, 0], top_edge[0, 0], left_edge[0, 0],
        site_tensor.reshape(phys * legs, legs),
        sketch[0, 0], grad_left[0, 0], grad_top[0, 0],
    )
    return (
        outs[0][None, None], outs[1][None, None], outs[2][None, None],
        outs[3].reshape(site_tensor.shape),
    )


def solution(mesh):
    edges = P("row", "col", None, None)
    site = P("row", "col", None, None, None, None, None)
    return jax.shard_map(
        local, mesh=mesh,
        in_specs=(edges, edges, edges, site, edges, edges, edges),
        out_specs=(edges, edges, edges, site),
        check_vma=False,
    )
```

profile of v0, /device:TPU:1, one launch (start us, length us, event | category | flops | bytes accessed | tf_op | source)
XLA Modules:
  0.0 40.6 jit_solution(16253226319468179683)
XLA Ops:
  0.6 0.0 copy-start.5
  0.6 0.9 %reshape.16.t_ref = bf16[32,16]{1,0:T(8,128)(2,1)S(1)} reshape(bf16[1,1,2,4,4,4,4]{6,5,4,3,2,1,0:T(4,128)(2,1)} %param.10) | data formatting | bytes 2048 | tf_op jit(solution)/shard_map/reshape | solution.py:277
  1.5 0.0 copy-done.5
  1.5 0.0 copy-start
  1.5 0.9 %copy-done = bf16[1,1,64,1024]{3,2,1,0:T(8,128)(2,1)S(1)} copy-done((bf16[1,1,64,1024]{3,2,1,0:T(8,128)(2,1)S(1)}, bf16[1,1,64,1024]{3,2,1,0:T(8,128)(2,1)}, u32[]{:S(2)}) %copy-start) | copy-done | bytes 131096
  2.4 0.0 copy-start.1
  2.4 0.9 %copy-done.1 = bf16[1,1,64,1024]{3,2,1,0:T(8,128)(2,1)S(1)} copy-done((bf16[1,1,64,1024]{3,2,1,0:T(8,128)(2,1)S(1)}, bf16[1,1,64,1024]{3,2,1,0:T(8,128)(2,1)}, u32[]{:S(2)}) %copy-start.1) | copy-done | bytes 131096
  3.3 0.0 copy-start.2
  3.3 0.9 %copy-done.2 = bf16[1,1,64,1024]{3,2,1,0:T(8,128)(2,1)S(1)} copy-done((bf16[1,1,64,1024]{3,2,1,0:T(8,128)(2,1)S(1)}, bf16[1,1,64,1024]{3,2,1,0:T(8,128)(2,1)}, u32[]{:S(2)}) %copy-start.2) | copy-done | bytes 131096
  4.2 0.0 copy-start.3
  4.2 0.9 %copy-done.3 = bf16[1,1,64,1024]{3,2,1,0:T(8,128)(2,1)S(1)} copy-done((bf16[1,1,64,1024]{3,2,1,0:T(8,128)(2,1)S(1)}, bf16[1,1,64,1024]{3,2,1,0:T(8,128)(2,1)}, u32[]{:S(2)}) %copy-start.3) | copy-done | bytes 131096
  5.1 0.0 copy-start.4
  5.1 0.9 %copy-done.4 = bf16[1,1,64,1024]{3,2,1,0:T(8,128)(2,1)S(1)} copy-done((bf16[1,1,64,1024]{3,2,1,0:T(8,128)(2,1)S(1)}, bf16[1,1,64,1024]{3,2,1,0:T(8,128)(2,1)}, u32[]{:S(2)}) %copy-start.4) | copy-done | bytes 131096
  6.0 31.9 %shard_map.102 = (bf16[64,64]{1,0:T(8,128)(2,1)S(1)}, bf16[64,1024]{1,0:T(8,128)(2,1)S(1)}, bf16[64,1024]{1,0:T(8,128)(2,1)S(1)}, f32[32,16]{1,0:T(8,128)S(1)}) custom-call(bf16[64,64]{1,0:T(8,128)(2,1)S(1)} %bitcast.16, bf16[64,1024]{1,0:T(8,128)(2,1)S(1)} %bitcast.11, bf16[64,1024]{1,0:T(8,128)(2,1)S(1)} %bitcast.12, bf16[32,16]{1,0:T(8,128)(2,1)S(1)} %reshape.16.t_ref, ...), custom_call_target="tpu_custom_call" | custom-call | tf_op jit(solution)/shard_map/pallas_call | solution.py:249
  37.9 0.7 %reshape.17 = f32[1,1,2,4,4,4,4]{6,5,4,3,2,1,0:T(4,128)} reshape(f32[32,16]{1,0:T(8,128)S(1)} %get-tuple-element.11) | data formatting | bytes 4096 | tf_op jit(solution)/shard_map/reshape | solution.py:282
  38.7 0.6 %copy.20 = bf16[1,1,64,64]{3,2,1,0:T(8,128)(2,1)} copy(bf16[1,1,64,64]{3,2,1,0:T(8,128)(2,1)S(1)} %bitcast.17) | data formatting | bytes 16384
  39.3 0.7 %copy.21 = bf16[1,1,64,1024]{3,2,1,0:T(8,128)(2,1)} copy(bf16[1,1,64,1024]{3,2,1,0:T(8,128)(2,1)S(1)} %bitcast.10) | data formatting | bytes 262144
  39.9 0.7 %copy.22 = bf16[1,1,64,1024]{3,2,1,0:T(8,128)(2,1)} copy(bf16[1,1,64,1024]{3,2,1,0:T(8,128)(2,1)S(1)} %bitcast.9) | data formatting | bytes 262144
Async XLA Ops:
  0.6 0.9 %copy-start.5 = (bf16[1,1,64,64]{3,2,1,0:T(8,128)(2,1)S(1)}, bf16[1,1,64,64]{3,2,1,0:T(8,128)(2,1)}, u32[]{:S(2)}) copy-start(bf16[1,1,64,64]{3,2,1,0:T(8,128)(2,1)} %param.7) | copy-start | bytes 24580
  1.5 0.9 %copy-start = (bf16[1,1,64,1024]{3,2,1,0:T(8,128)(2,1)S(1)}, bf16[1,1,64,1024]{3,2,1,0:T(8,128)(2,1)}, u32[]{:S(2)}) copy-start(bf16[1,1,64,1024]{3,2,1,0:T(8,128)(2,1)} %param.8) | copy-start | bytes 393220
  2.4 0.9 %copy-start.1 = (bf16[1,1,64,1024]{3,2,1,0:T(8,128)(2,1)S(1)}, bf16[1,1,64,1024]{3,2,1,0:T(8,128)(2,1)}, u32[]{:S(2)}) copy-start(bf16[1,1,64,1024]{3,2,1,0:T(8,128)(2,1)} %param.9) | copy-start | bytes 393220
  3.3 0.9 %copy-start.2 = (bf16[1,1,64,1024]{3,2,1,0:T(8,128)(2,1)S(1)}, bf16[1,1,64,1024]{3,2,1,0:T(8,128)(2,1)}, u32[]{:S(2)}) copy-start(bf16[1,1,64,1024]{3,2,1,0:T(8,128)(2,1)} %param.11) | copy-start | bytes 393220
  4.2 0.9 %copy-start.3 = (bf16[1,1,64,1024]{3,2,1,0:T(8,128)(2,1)S(1)}, bf16[1,1,64,1024]{3,2,1,0:T(8,128)(2,1)}, u32[]{:S(2)}) copy-start(bf16[1,1,64,1024]{3,2,1,0:T(8,128)(2,1)} %param.12) | copy-start | bytes 393220
  5.1 0.9 %copy-start.4 = (bf16[1,1,64,1024]{3,2,1,0:T(8,128)(2,1)S(1)}, bf16[1,1,64,1024]{3,2,1,0:T(8,128)(2,1)}, u32[]{:S(2)}) copy-start(bf16[1,1,64,1024]{3,2,1,0:T(8,128)(2,1)} %param.13) | copy-start | bytes 393220
where the time goes:
time: 40.9 us; the launch traced here: 40.6 us
  Pallas kernels  31.9 us (78%)
  local copies, waits for them, and re-layouts  8.01 us (20%)
  between operations  0.67 us (2%)
    pallas_call x1, Pallas kernels, local(): pl.pallas_call(functools.partial(kernel, (chi, bond, phys, 8)), out_shape...  31.9 us
    unnamed x15, local copies, waits for them, and re-layouts  6.43 us
    reshape x1, local copies, waits for them, and re-layouts, local(): site_tensor.reshape(phys * legs, legs)  0.85 us

commit v1 on v0

--- a/solution.py
+++ b/solution.py
@@ -90,11 +90,12 @@
 
 
 def picks(bond, which, across):
+    full = bond**4
     legs = bond * bond
-    full = legs * legs
-    shape = (legs, full) if across else (full, legs)
+    tall = bond**3
+    shape = (tall, full) if across else (full, tall)
     r = lax.broadcasted_iota(jnp.int32, shape, 1 if across else 0)
-    key = lax.broadcasted_iota(jnp.int32, shape, 0 if across else 1)
+    key = lax.broadcasted_iota(jnp.int32, shape, 0 if across else 1) // bond
     hi, lo = r // legs, lax.rem(r, legs)
     if which == 0:
         got = (hi // bond) * bond + lo // bond
@@ -103,20 +104,37 @@
     return jnp.where(got == key, 1.0, 0.0).astype(BF16)
 
 
+def picks_last(bond, which, across):
+    full = bond**4
+    shape = (bond, full) if across else (full, bond)
+    r = lax.broadcasted_iota(jnp.int32, shape, 1 if across else 0)
+    key = lax.broadcasted_iota(jnp.int32, shape, 0 if across else 1)
+    lo = lax.rem(r, bond * bond)
+    got = lo // bond if which == 0 else lax.rem(lo, bond)
+    return jnp.where(got == key, 1.0, 0.0).astype(BF16)
+
+
+def same_v(bond, which):
+    shape = (bond**3, bond**4)
+    v = lax.rem(lax.broadcasted_iota(jnp.int32, shape, 0), bond)
+    hi = lax.broadcasted_iota(jnp.int32, shape, 1) // (bond * bond)
+    return v == (hi // bond if which == 0 else lax.rem(hi, bond))
+
+
 def kernel(
     sizes,
     c_ref, u_ref, l_ref, t_ref, sk_ref, gl_ref, gt_ref,
     corner_out, top_out, left_out, site_out,
     lp_own, lp, top_in, corner_in,
-    sk_p, sk_n, right_p, down_p,
+    sk_p, right_p, down_p,
     skr_in, skb_in, right_in, down_in,
     dtop, dcorner, dleft,
-    dtop_in, dcorner_in, dleft_in,
     scr, fbd, rf, lf, a_ref, at_ref, layer,
     secb, qrows, dqb, dsrows,
-    send, recv,
+    l_in, sk_in, gl_in, gt_in,
+    send, recv, loads,
 ):
-    chi, bond, phys, chunk = sizes
+    chi, bond, phys, steps = sizes
     legs = bond * bond
     two = 2 * chi
     half = chi // 2
@@ -129,7 +147,16 @@
     others = ((rn, c), (rp, c), (r, cn), (r, cp), (rn, cn), (rp, cp))
     for other in others:
         pl.semaphore_signal(barrier, inc=1, device_id=other, device_id_type=MESH)
-    lp_own[...] = edge_rows(l_ref[...], scr, legs, chi).astype(BF16)
+    fetch = [
+        pltpu.make_async_copy(src, dst, loads.at[n])
+        for n, (src, dst) in enumerate(
+            ((l_ref, l_in), (gt_ref, gt_in), (sk_ref, sk_in), (gl_ref, gl_in))
+        )
+    ]
+    for copy in fetch:
+        copy.start()
+    fetch[0].wait()
+    lp_own[...] = edge_rows(l_in[...], scr, legs, chi).astype(BF16)
     pl.semaphore_wait(barrier, len(others))
 
     def put(n, src, dst, to):
@@ -145,18 +172,28 @@
     left_copy = put(2, lp_own, lp, (r, cn))
 
     for p in range(phys):
-        site = t_ref[p * legs : (p + 1) * legs, :]
+        site = jnp.concatenate(
+            [
+                t_ref[0, 0, p, u, w].astype(F32)
+                for u in range(bond)
+                for w in range(bond)
+            ],
+            axis=0,
+        ).astype(BF16)
         for which in range(2):
-            wide = mm(site, picks(bond, which, True)).astype(BF16)
+            wide = mm(site, picks_last(bond, which, True))
+            wide = jnp.where(same_v(bond, which), wide, 0.0).astype(BF16)
             layer[p, which] = mm(picks(bond, which, False), wide).astype(BF16)
     double = sum(
         layer[p, 0].astype(F32) * layer[p, 1].astype(F32) for p in range(phys)
     )
     at_ref[...] = double.astype(BF16)
     a_ref[...] = double.T.astype(BF16)
-    spread(gt_ref[...], rf, two, legs, chi)
-    spread(sk_ref[...], rf, 2 * two, legs, chi)
-    glp = edge_rows(gl_ref[...], scr, legs, chi)
+    for copy in fetch[1:]:
+        copy.wait()
+    spread(gt_in[...], rf, two, legs, chi)
+    spread(sk_in[...], rf, 2 * two, legs, chi)
+    glp = edge_rows(gl_in[...], scr, legs, chi)
     lf[:, :two] = glp.astype(BF16)
     glp_t = glp.T.astype(BF16)
 
@@ -166,70 +203,73 @@
     spread(first, fbd, 0, legs, chi)
     left_copy.wait()
 
-    rows_step = chunk * legs
-    lanes_step = chunk * two
-    steps = half // chunk
-
-    @pl.loop(0, steps)
-    def _(n):
-        rows = pl.ds(pl.multiple_of(n * rows_step, rows_step), rows_step)
-        lanes = pl.ds(pl.multiple_of(n * lanes_step, lanes_step), lanes_step)
+    rows_step = half * legs // steps
+    lanes_step = half * two // steps
+    parts = [
+        (slice(n * rows_step, (n + 1) * rows_step), slice(n * lanes_step, (n + 1) * lanes_step))
+        for n in range(steps)
+    ]
+
+    skb_copies, skr_copies, right_copies = [], [], []
+    for n, (rows, lanes) in enumerate(parts):
         block = to_blocks(mm(lp[rows, :], fbd[...]).astype(BF16), legs, two)
         secb[:, lanes] = block
-        qrows[rows, :] = to_rows(mm(a_ref[...], block).astype(BF16), legs, two)
-
-    both = mm_nt(qrows[...], rf[two:, :]).astype(BF16)
-    right_p[...] = both[:, :two]
-    sk_p[...] = both[:, two:]
-    skr_copy = put(3, sk_p, skr_in, (r, cp))
-    right_copy = put(5, right_p, right_in, (r, cn))
-    sk_n[...] = edge_lanes(both[:, two:].astype(F32), scr, legs, chi).astype(BF16)
-    skb_copy = put(4, sk_n, skb_in, (rp, c))
+        quad = to_rows(mm(a_ref[...], block).astype(BF16), legs, two)
+        qrows[rows, :] = quad
+        both = mm_nt(quad, rf[two:, :]).astype(BF16)
+        sk_p[rows, :] = both[:, two:]
+        right_p[rows, :] = both[:, :two]
+        at = 6 + 3 * n
+        skb_copies.append(put(at, sk_p.at[rows], skb_in.at[rows], (rp, c)))
+        skr_copies.append(put(at + 1, sk_p.at[rows], skr_in.at[rows], (r, cp)))
+        right_copies.append(put(at + 2, right_p.at[rows], right_in.at[rows], (r, cn)))
+
     down = gather_diag(mm(glp_t, qrows[...]), legs, chi).astype(BF16)
     down_p[...] = edge_rows(down, scr, legs, chi).astype(BF16)
-    down_copy = put(6, down_p, down_in, (rn, c))
+    down_copy = put(3, down_p, down_in, (rn, c))
 
     lp_t = lp[...].astype(F32).T.astype(BF16)
-    skr_copy.wait()
+    for copy in skr_copies:
+        copy.wait()
     lf[:, two : 2 * two] = skr_in[...]
-    skb_copy.wait()
-    spread(skb_in[...], rf, 0, legs, chi)
-    right_copy.wait()
+    for copy in skb_copies:
+        copy.wait()
+    spread(edge_lanes(skb_in[...].astype(F32), scr, legs, chi), rf, 0, legs, chi)
+    for copy in right_copies:
+        copy.wait()
     down_copy.wait()
     lf[:, 2 * two :] = (down_in[...].astype(F32) + right_in[...].astype(F32)).astype(BF16)
 
-    @pl.loop(0, steps)
-    def _(n):
-        rows = pl.ds(pl.multiple_of(n * rows_step, rows_step), rows_step)
-        lanes = pl.ds(pl.multiple_of(n * lanes_step, lanes_step), lanes_step)
+    for rows, lanes in parts:
         block = to_blocks(mm(lf[rows, :], rf[...]).astype(BF16), legs, two)
         dqb[:, lanes] = block
         dsrows[rows, :] = to_rows(mm(at_ref[...], block).astype(BF16), legs, two)
 
     dfirst = gather_diag(mm(lp_t, dsrows[...]), legs, chi).astype(BF16)
     dtop[...] = mm(corner_in[...].astype(F32).T.astype(BF16), dfirst).astype(BF16)
-    dtop_copy = put(7, dtop, dtop_in, (rp, c))
+    dtop_copy = put(4, dtop, top_out, (rp, c))
     dcorner[...] = mm_nt(dfirst, top_in[...]).astype(BF16)
-    dcorner_copy = put(8, dcorner, dcorner_in, (rp, cp))
+    dcorner_copy = put(5, dcorner, corner_out, (rp, cp))
     dleft[...] = edge_lanes(mm_nt(dsrows[...], fbd[...]), scr, legs, chi).astype(BF16)
-    dleft_copy = put(9, dleft, dleft_in, (r, cp))
+    dleft_copy = put(6 + 3 * steps, dleft, left_out, (r, cp))
 
     ddouble = mm_nt(secb[...], dqb[...])
     for p in range(phys):
         total = None
         for which in range(2):
             part = (ddouble * layer[p, 1 - which].astype(F32)).astype(BF16)
-            part = mm(picks(bond, which, True), part).astype(BF16)
-            part = mm(part, picks(bond, which, False))
+            part = mm(picks(bond, which, True), part)
+            part = jnp.where(same_v(bond, which), part, 0.0).astype(BF16)
+            part = mm(part, picks_last(bond, which, False))
             total = part if total is None else total + part
-        site_out[p * legs : (p + 1) * legs, :] = total
+        for u in range(bond):
+            for w in range(bond):
+                at = (u * bond + w) * bond
+                site_out[0, 0, p, u, w] = total[at : at + bond, :]
 
     dtop_copy.wait()
-    top_out[...] = dtop_in[...]
     dcorner_copy.wait()
-    corner_out[...] = dcorner_in[...]
     dleft_copy.wait()
-    left_out[...] = dleft_in[...]
 
 
 def local(corner, top_edge, left_edge, site_tensor, sketch, grad_left, grad_top):
@@ -237,6 +277,7 @@
     phys, bond = site_tensor.shape[2:4]
     legs = bond * bond
     width = legs * chi
+    steps = 2
     two = 2 * chi
     rows = legs * chi // 2
     wide = legs * two
@@ -246,40 +287,42 @@
     packed = vm(rows, two)
     tile = vm(chi, chi)
     spec = pl.BlockSpec(memory_space=pltpu.VMEM)
+    hbm = pl.BlockSpec(memory_space=pltpu.HBM)
     outs = pl.pallas_call(
-        functools.partial(kernel, (chi, bond, phys, 8)),
+        functools.partial(kernel, (chi, bond, phys, steps)),
         out_shape=(
             jax.ShapeDtypeStruct((chi, chi), BF16),
             jax.ShapeDtypeStruct((chi, width), BF16),
             jax.ShapeDtypeStruct((chi, width), BF16),
-            jax.ShapeDtypeStruct((phys * legs, legs), F32),
+            jax.ShapeDtypeStruct(site_tensor.shape, F32),
         ),
-        in_specs=[spec] * 7,
+        in_specs=[hbm, hbm, hbm, spec, hbm, hbm, hbm],
         out_specs=(spec,) * 4,
         scratch_shapes=[
             packed, packed, edge, tile,
-            packed, edge, packed, packed,
-            packed, edge, packed, packed,
-            edge, tile, edge,
+            packed, packed, packed,
+            packed, packed, packed, packed,
             edge, tile, edge,
             pltpu.VMEM((width, two), F32),
             vm(two, wide), vm(3 * two, wide), vm(rows, 3 * two),
             vm(full, full), vm(full, full), vm(phys, 2, full, full),
             vm(full, rows * two // legs), vm(rows, wide), vm(full, rows * two // legs), vm(rows, wide),
-            pltpu.SemaphoreType.DMA((10,)),
-            pltpu.SemaphoreType.DMA((10,)),
+            edge, edge, edge, edge,
+            pltpu.SemaphoreType.DMA((7 + 3 * steps,)),
+            pltpu.SemaphoreType.DMA((7 + 3 * steps,)),
+            pltpu.SemaphoreType.DMA((4,)),
         ],
         compiler_params=pltpu.CompilerParams(
-            collective_id=0, has_side_effects=True, vmem_limit_bytes=48 * 1024 * 1024
+            collective_id=0, has_side_effects=True, vmem_limit_bytes=60 * 1024 * 1024
         ),
     )(
         corner[0, 0], top_edge[0, 0], left_edge[0, 0],
-        site_tensor.reshape(phys * legs, legs),
+        site_tensor,
         sketch[0, 0], grad_left[0, 0], grad_top[0, 0],
     )
     return (
         outs[0][None, None], outs[1][None, None], outs[2][None, None],
-        outs[3].reshape(site_tensor.shape),
+        outs[3],
     )
 
 

time: 40.9 us -> 36.5 us (0.89)
  local copies, waits for them, and re-layouts: 8.01 us -> 4.42 us
  Pallas kernels: 31.9 us -> 31.1 us
    unnamed x15 -> x8, local copies, waits for them, and re-layouts: 6.43 us -> 4.42 us
    reshape x2 -> x0, local copies, waits for them, and re-layouts: 1.58 us -> none  [the longest x1 0.85 us: local(): site_tensor.reshape(phys * legs, legs)]
    pallas_call x1, Pallas kernels: 31.9 us -> 31.1 us  [local(): pl.pallas_call(functools.partial(kernel, (chi, bond, phys, steps)), out_s...]
where the time goes in v1:
time: 36.5 us; the launch traced here: 36.2 us
  Pallas kernels  31.1 us (85%)
  local copies, waits for them, and re-layouts  4.42 us (12%)
  between operations  0.64 us (2%)
    pallas_call x1, Pallas kernels, local(): pl.pallas_call(functools.partial(kernel, (chi, bond, phys, steps)), out_s...  31.1 us
    unnamed x8, local copies, waits for them, and re-layouts  4.42 us

profile of v1, /device:TPU:1, one launch (start us, length us, event | category | flops | bytes accessed | tf_op | source)
XLA Modules:
  0.0 36.2 jit_solution(15581783226779594294)
XLA Ops:
  0.6 31.1 %shard_map.102 = (bf16[64,64]{1,0:T(8,128)(2,1)}, bf16[64,1024]{1,0:T(8,128)(2,1)}, bf16[64,1024]{1,0:T(8,128)(2,1)}, f32[1,1,2,4,4,4,4]{6,5,4,3,2,1,0:T(4,128)}) custom-call(bf16[64,64]{1,0:T(8,128)(2,1)} %bitcast.16, bf16[64,1024]{1,0:T(8,128)(2,1)} %bitcast.11, bf16[64,1024]{1,0:T(8,128)(2,1)} %bitcast.12, bf16[1,1,2,4,4,4,4]{6,5,4,3,2,1,0:T(4,128)(2,1)} %t_ref.1, ...), custom_call_target="tpu_custom_call" | custom-call | tf_op jit(solution)/shard_map/pallas_call | solution.py:291
  31.8 1.3 %copy.15 = bf16[1,1,64,64]{3,2,1,0:T(8,128)(2,1)} copy(bf16[1,1,64,64]{3,2,1,0:T(8,128)(2,1)} %bitcast.17) | data formatting | bytes 16384
  33.1 0.0 copy-start
  33.1 1.6 %copy.16 = bf16[1,1,64,1024]{3,2,1,0:T(8,128)(2,1)} copy(bf16[1,1,64,1024]{3,2,1,0:T(8,128)(2,1)} %bitcast.10) | data formatting | bytes 262144
  34.7 0.0 copy-done
  34.7 0.0 copy-start.1
  34.7 0.7 %copy.17 = bf16[1,1,64,1024]{3,2,1,0:T(8,128)(2,1)} copy(bf16[1,1,64,1024]{3,2,1,0:T(8,128)(2,1)S(1)} %bitcast.9) | data formatting | bytes 262144
  35.3 0.2 copy-done.1
  35.6 0.6 %copy.18 = f32[1,1,2,4,4,4,4]{6,5,4,3,2,1,0:T(4,128)} copy(f32[1,1,2,4,4,4,4]{6,5,4,3,2,1,0:T(4,128)S(1)} %copy-done.1) | data formatting | bytes 4096
Async XLA Ops:
  33.1 1.6 %copy-start = (bf16[64,1024]{1,0:T(8,128)(2,1)S(1)}, bf16[64,1024]{1,0:T(8,128)(2,1)}, u32[]{:S(2)}) copy-start(bf16[64,1024]{1,0:T(8,128)(2,1)} %get-tuple-element.10) | copy-start | bytes 393220
  34.7 0.9 %copy-start.1 = (f32[1,1,2,4,4,4,4]{6,5,4,3,2,1,0:T(4,128)S(1)}, f32[1,1,2,4,4,4,4]{6,5,4,3,2,1,0:T(4,128)}, u32[]{:S(2)}) copy-start(f32[1,1,2,4,4,4,4]{6,5,4,3,2,1,0:T(4,128)} %get-tuple-element.19) | copy-start | bytes 6148
